TPU v7x, 512 devices: a whole 4x4x16 slice. The times are simulated.
512 devices in a mesh: layer: 8 (over y, core), feat: 16 (over z_hi, x), width: 4 (over z_lo).
Axes of the slice: x: 4, y: 4, z: 16 (z_hi: 4, z_lo: 4; z = z_hi * 4 + z_lo), core: 2. Of those that a mesh axis runs over, the one named last changes fastest.
Arguments:
- resid: bfloat16 [2, 128, 2048], P(None, 'layer', 'width'), may hold values from -6 to 6
- enc_w: bfloat16 [2, 2048, 65536], P(None, 'width', ('layer', 'feat')), may hold values from -0.125 to 0.125
- enc_b: float32 [2, 65536], P(None, ('layer', 'feat')), may hold values from -3 to 3
- dec_w: float32 [3, 65536, 2048], P(None, ('layer', 'feat'), 'width'), may hold values from -0.09375 to 0.09375
- dec_b: float32 [2, 2048], P(None, 'width'), may hold values from -2 to 2
- target: float32 [2, 128, 2048], P(None, ('layer', 'feat'), 'width'), may hold values from -6 to 6
Outputs:
- recon: float32 [2, 128, 2048], P(None, ('layer', 'feat'), 'width')
- err: float32 [2, 128], P(None, ('layer', 'feat'))
All inputs are finite; a program needn't handle non-finite values.
Results may differ from a plain program's by a relative error of at most 0.00035.
Values may be sent and summed in bfloat16 or wider, within the bound.
A program may use at most 64 MiB of HBM per device.

v0:
```python
import jax
import jax.numpy as jnp
from jax import lax
from jax.sharding import PartitionSpec as P


def decode_rows(act, dec_w, target_idx):
    total = None
    for layer_idx in range(target_idx + 1):
        block = target_idx * (target_idx + 1) // 2 + layer_idx
        rows = act[layer_idx]
        term = jnp.dot(
            rows, dec_w[block], precision=lax.Precision.HIGHEST, preferred_element_type=jnp.float32
        )
        total = term if total is None else total + term
    return total


def per_device(resid, enc_w, enc_b, dec_w, dec_b, target):
    layers = resid.shape[0]
    gathered = lax.all_gather(resid, "layer", axis=1, tiled=True)
    tokens = gathered.shape[1]
    partial_pre = jnp.einsum("ltd,ldf->ltf", gathered, enc_w, preferred_element_type=jnp.float32)
    pre = lax.psum(partial_pre, "width")
    act = jnp.maximum(pre + enc_b[:, None, :], 0.0)
    own_rows = tokens // lax.axis_size(("layer", "feat"))
    pieces = []
    for target_idx in range(layers):

        def decode_single(start, count, target_idx=target_idx):
            return decode_rows(act, dec_w, target_idx)

        pieces.append(
            lax.psum_scatter(
                decode_single(jnp.int32(0), own_rows * lax.axis_size(("layer", "feat"))),
                ("layer", "feat"),
                scatter_dimension=0,
                tiled=True,
            )
        )
    summed = jnp.stack(pieces, 0)
    recon = summed + dec_b[:, None, :]
    diff = recon - target
    sq_error, sq_target = lax.psum(
        (jnp.sum(diff * diff, axis=2), jnp.sum(target * target, axis=2)), "width"
    )
    err = sq_error / (sq_target + 1e-06)
    return (recon, err)


def solution(mesh):
    in_specs = (
        P(None, "layer", "width"),
        P(None, "width", ("layer", "feat")),
        P(None, ("layer", "feat")),
        P(None, ("layer", "feat"), "width"),
        P(None, "width"),
        P(None, ("layer", "feat"), "width"),
    )
    out_specs = (P(None, ("layer", "feat"), "width"), P(None, ("layer", "feat")))
    return jax.shard_map(
        per_device, mesh=mesh, in_specs=in_specs, out_specs=out_specs, check_vma=False
    )
```

profile of v0, /device:TPU:32, one launch (start us, length us, event | category | flops | bytes accessed | tf_op | source)
XLA Modules:
  0.0 1588.4 jit_solution(10520074433764686368)
XLA Ops:
  7.2 0.0 copy-start
  7.2 0.0 all-reduce.7.cloned.1.call-start
  7.2 13.7 all_gather.3
  20.9 0.0 copy-done
  20.9 1.1 fusion.12
  22.1 0.0 all-reduce.7.cloned.1.call-update
  22.1 0.0 copy-start.1
  22.1 0.0 copy-start.2
  22.1 0.0 all-reduce.9.cloned.1.call-start
  22.2 64.1 %all-reduce.7.cloned.1.call-done = f32[2,128,512]{2,1,0:T(8,128)} async-done(((f32[2,128,512]{2,1,0:T(8,128)}), f32[2,128,512]{2,1,0:T(8,128)}) %all-reduce.7.cloned.1.call-update) | async-done | bytes 524304 | tf_op jit(solution)/shard_map/psum | solution.py:24
  86.2 1.1 add_maximum_fusion
  87.3 1.9 fusion.1
  89.3 2.7 fusion.3
  91.9 2.6 convolution_add_fusion
  94.6 0.0 all-reduce.9.cloned.1.call-update
  94.6 1.3 dynamic-slice
  95.9 0.0 copy-done.1
  95.9 0.1 multiply_reduce_fusion
  96.0 1473.3 %all-reduce.9.cloned.1.call-done = (f32[128,512]{1,0:T(8,128)}, f32[128,512]{1,0:T(8,128)}) async-done(((f32[128,512]{1,0:T(8,128)}, f32[128,512]{1,0:T(8,128)}), (f32[128,512]{1,0:T(8,128)}, f32[128,512]{1,0:T(8,128)})) %all-reduce.9.cloned.1.call-update) | async-done | bytes 524304
  1569.3 1.4 constant_dynamic-slice_fusion
  1570.7 0.0 copy-done.2
  1570.7 0.1 fusion.10
  1570.8 0.6 copy.11
  1571.4 9.7 all-reduce.3
  1581.1 0.5 add_divide_fusion
Async XLA Ops:
  7.2 13.8 copy-start
  7.2 79.0 %all-reduce.7.cloned.1.call-start = ((), (), s32[]{:S(2)}) async-start(), calls=%async_computation | async-start | bytes 1048576 | tf_op jit(solution)/shard_map/psum | solution.py:24
  22.1 73.8 %copy-start.1 = (f32[2,1,512]{2,1,0:T(1,128)S(1)}, f32[2,1,512]{2,1,0:T(1,128)}, u32[]{:S(2)}) copy-start(f32[2,1,512]{2,1,0:T(1,128)} %param.11) | copy-start | bytes 12292
  22.1 1548.6 %copy-start.2 = (f32[2,512]{1,0:T(2,128)S(1)}, f32[2,512]{1,0:T(2,128)}, u32[]{:S(2)}) copy-start(f32[2,512]{1,0:T(2,128)} %param.10) | copy-start | bytes 12292
  22.1 1547.2 %all-reduce.9.cloned.1.call-start = ((), (), s32[]{:S(2)}) async-start(), calls=%async_computation.1 | async-start | bytes 1048576
Sparse Core Ops, SparseCore 0:
  22.2 63.9 all-reduce.6
  94.7 1474.5 all-reduce.8
where the time goes:
time: 1590 us
  waiting for transfers between devices  1540 us (97%)
  blocking collectives  23.4 us (1%)
    unnamed x3, waiting for transfers between devices  1470 us
    psum x1, waiting for transfers between devices, per_device(): pre = lax.psum(partial_pre, 'width')  64.1 us
  transfers between devices with their start and end apart: 2, of which 2 were waited for; matrix products, arithmetic and copies ran while one was open for 0% of the time, Pallas kernels for 0%

commit v1 on v0

--- a/solution.py
+++ b/solution.py
@@ -21,7 +21,7 @@
     gathered = lax.all_gather(resid, "layer", axis=1, tiled=True)
     tokens = gathered.shape[1]
     partial_pre = jnp.einsum("ltd,ldf->ltf", gathered, enc_w, preferred_element_type=jnp.float32)
-    pre = lax.psum(partial_pre, "width")
+    pre = lax.all_gather(partial_pre, axis_name="width").sum(axis=0)
     act = jnp.maximum(pre + enc_b[:, None, :], 0.0)
     own_rows = tokens // lax.axis_size(("layer", "feat"))
     pieces = []

time: 1590 us -> 1580 us (level)
    psum x1 -> x0, waiting for transfers between devices: 64.1 us -> none  [per_device(): pre = lax.psum(partial_pre, 'width')]
    all_gather x0 -> x1, waiting for transfers between devices: none -> 58 us  [per_device(): pre = lax.all_gather(partial_pre, axis_name='width').sum(axis=0)]
where the time goes in v1:
time: 1580 us
  waiting for transfers between devices  1530 us (97%)
  blocking collectives  23.4 us (1%)
    unnamed x3, waiting for transfers between devices  1470 us
    all_gather x1, waiting for transfers between devices, per_device(): pre = lax.all_gather(partial_pre, axis_name='width').sum(axis=0)  58 us
  transfers between devices with their start and end apart: 2, of which 2 were waited for; matrix products, arithmetic and copies ran while one was open for 0% of the time, Pallas kernels for 0%

profile of v1, /device:TPU:32, one launch (start us, length us, event | category | flops | bytes accessed | tf_op | source)
XLA Modules:
  0.0 1583.2 jit_solution(6761668942352303609)
XLA Ops:
  7.2 0.0 copy-start
  7.2 0.0 copy-start.2
  7.2 0.0 all-gather.3.cloned.1.call-start
  7.2 13.7 all_gather.9
  20.9 0.0 copy-done
  20.9 1.1 fusion.12
  22.0 0.0 all-gather.3.cloned.1.call-update
  22.1 0.0 all-reduce.6.cloned.1.call-start
  22.1 58.0 %all-gather.3.cloned.1.call-done = f32[8,128,512]{2,1,0:T(8,128)} async-done(((f32[2,128,512]{2,1,0:T(8,128)}), f32[8,128,512]{2,1,0:T(8,128)}) %all-gather.3.cloned.1.call-update) | async-done | bytes 2097168 | tf_op jit(solution)/shard_map/all_gather | solution.py:24
  80.2 1.9 reduce_sum.31
  82.0 0.0 copy-done.2
  82.0 0.0 copy-start.1
  82.0 0.0 copy-start.3
  82.1 0.1 add_maximum_fusion
  82.1 1.9 fusion.1
  84.1 2.6 fusion.3
  86.7 2.6 convolution_add_fusion
  89.4 0.0 all-reduce.6.cloned.1.call-update
  89.4 1.3 dynamic-slice
  90.7 0.0 copy-done.1
  90.7 0.1 multiply_reduce_fusion
  90.8 1473.3 %all-reduce.6.cloned.1.call-done = (f32[128,512]{1,0:T(8,128)}, f32[128,512]{1,0:T(8,128)}) async-done(((f32[128,512]{1,0:T(8,128)}, f32[128,512]{1,0:T(8,128)}), (f32[128,512]{1,0:T(8,128)}, f32[128,512]{1,0:T(8,128)})) %all-reduce.6.cloned.1.call-update) | async-done | bytes 524304
  1564.0 1.4 constant_dynamic-slice_fusion
  1565.4 0.0 copy-done.3
  1565.4 0.1 fusion.10
  1565.6 0.6 copy.11
  1566.2 9.7 all-reduce.3
  1575.8 0.5 add_divide_fusion
Async XLA Ops:
  7.2 13.8 copy-start
  7.2 74.8 %copy-start.2 = (f32[2,512]{1,0:T(2,128)S(1)}, f32[2,512]{1,0:T(2,128)}, u32[]{:S(2)}) copy-start(f32[2,512]{1,0:T(2,128)} %param.8) | copy-start | bytes 12292
  7.2 73.0 %all-gather.3.cloned.1.call-start = ((), (), s32[]{:S(2)}) async-start(), calls=%async_computation | async-start | bytes 2621440 | tf_op jit(solution)/shard_map/all_gather | solution.py:24
  22.1 1542.0 %all-reduce.6.cloned.1.call-start = ((), (), s32[]{:S(2)}) async-start(), calls=%async_computation.1 | async-start | bytes 1048576
  82.0 8.6 copy-start.1
  82.0 1483.4 %copy-start.3 = (f32[2,512]{1,0:T(2,128)S(1)}, f32[2,512]{1,0:T(2,128)}, u32[]{:S(2)}) copy-start(f32[2,512]{1,0:T(2,128)} %param.10) | copy-start | bytes 12292
Sparse Core Ops, SparseCore 0:
  22.2 57.9 all-gather.2
  89.5 1474.4 all-reduce.5
